TPU v7x, 32 devices: a whole 2x2x4 slice. The times are simulated.
32 devices in a mesh: section: 2 (over core), dp: 4 (over y, x), seq: 4 (over z).
Axes of the slice: x: 2, y: 2, z: 4, core: 2. Of those that a mesh axis runs over, the one named last changes fastest.
Arguments:
- inputs: bfloat16 [2, 4, 1280, 1024], P(None, 'dp', 'seq'), may hold values from -6 to 6
- cotangent: bfloat16 [2, 4, 1280, 1024], P(None, 'dp', 'seq'), may hold values from -6 to 6
- view_tokens: int32 [2, 4, 6], P(None, 'dp'), may hold values from 0 to 128, as said below
- ln1_gain: bfloat16 [2, 1024], P('section'), may hold values from 0.099609375 to 1.8984375
- ln1_bias: bfloat16 [2, 1024], P('section'), may hold values from -3 to 3
- w_qkv: bfloat16 [2, 1024, 3072], P('section'), may hold values from -0.1875 to 0.1875
- b_query: bfloat16 [2, 1024], P('section'), may hold values from -3 to 3
- b_value: bfloat16 [2, 1024], P('section'), may hold values from -0.29882812 to 0.29882812
- w_out: bfloat16 [2, 1024, 1024], P('section'), may hold values from -3 to 3
- b_out: bfloat16 [2, 1024], P('section'), may hold values from -3 to 3
- ln2_gain: bfloat16 [2, 1024], P('section'), may hold values from 0.099609375 to 1.8984375
- ln2_bias: bfloat16 [2, 1024], P('section'), may hold values from -3 to 3
- w_up: bfloat16 [2, 1024, 4096], P('section'), may hold values from -0.1875 to 0.1875
- b_up: bfloat16 [2, 4096], P('section'), may hold values from -3 to 3
- w_down: bfloat16 [2, 4096, 1024], P('section'), may hold values from -0.09375 to 0.09375
- b_down: bfloat16 [2, 1024], P('section'), may hold values from -3 to 3
Outputs:
- activations: bfloat16 [2, 2, 4, 1280, 1024], P('section', None, 'dp', 'seq')
- input_grad: bfloat16 [2, 2, 4, 1280, 1024], P('section', None, 'dp', 'seq')
- g_ln1_gain: float32 [2, 1024], P('section', ('dp', 'seq'))
- g_ln1_bias: float32 [2, 1024], P('section', ('dp', 'seq'))
- g_w_qkv: float32 [2, 1024, 3072], P('section', None, ('dp', 'seq'))
- g_b_query: float32 [2, 1024], P('section', ('dp', 'seq'))
- g_b_value: float32 [2, 1024], P('section', ('dp', 'seq'))
- g_w_out: float32 [2, 1024, 1024], P('section', None, ('dp', 'seq'))
- g_b_out: float32 [2, 1024], P('section', ('dp', 'seq'))
- g_ln2_gain: float32 [2, 1024], P('section', ('dp', 'seq'))
- g_ln2_bias: float32 [2, 1024], P('section', ('dp', 'seq'))
- g_w_up: float32 [2, 1024, 4096], P('section', None, ('dp', 'seq'))
- g_b_up: float32 [2, 4096], P('section', ('dp', 'seq'))
- g_w_down: float32 [2, 4096, 1024], P('section', None, ('dp', 'seq'))
- g_b_down: float32 [2, 1024], P('section', ('dp', 'seq'))
Inputs may be any that keep to these rules, and one draw needn't show every extreme that they name: view_tokens[m, s, i] counts the valid tokens of view i of scene s in micro-batch m; its 128 slots follow the 512 triplane tokens and the slots of earlier views, and its valid tokens come first. A scene has 2 to 6 views, which take the first slots; a present view has 32 to 128 valid tokens, the first view of each scene exactly 128; absent views hold 0.
All inputs are finite; a program needn't handle non-finite values.
Results may differ from a plain program's by a relative error of at most 0.015.
Values may be sent and summed in bfloat16 or wider, within the bound.
A program may use at most 448 MiB of HBM per device.

v0:
```python
import functools
import math

import jax
import jax.numpy as jnp
from jax import lax
from jax.experimental import pallas as pl
from jax.experimental.pallas import tpu as pltpu
from jax.sharding import PartitionSpec as P

D = 1024
H = 16
DH = 64
FF = 4096
VIEWS = 6
TRI = 512
VSLOT = 128
MICRO = 2
LEN = 1280
BQ = 256
NCH = 8
FC = FF // NCH
NCHF = 4
FCF = FF // NCHF
SCALE2 = DH ** (-0.5) * math.log2(math.e)
F32 = jnp.float32
BF16 = jnp.bfloat16
VMEM_LIMIT = 56 * 2**20


def params():
    return pltpu.CompilerParams(vmem_limit_bytes=VMEM_LIMIT)


def mm(a, b):
    return lax.dot_general(a, b, (((1,), (0,)), ((), ())), preferred_element_type=F32)


def mm_nt(a, b):
    return lax.dot_general(a, b, (((1,), (1,)), ((), ())), preferred_element_type=F32)


def mm_tn(a, b):
    return lax.dot_general(a, b, (((0,), (0,)), ((), ())), preferred_element_type=F32)


def norm_stats(values):
    average = jnp.mean(values, axis=-1, keepdims=True)
    centered = values - average
    variance = jnp.mean(centered * centered, axis=-1, keepdims=True)
    inverse = lax.rsqrt(variance + 1e-05)
    return centered * inverse, inverse


def head_lanes(shape, head):
    lane = lax.broadcasted_iota(jnp.int32, shape, 1)
    return (lane >= head * DH) & (lane < (head + 1) * DH)


def shards_of():
    return lax.axis_size("dp") * lax.axis_size("seq")


def split_halves(value, unit, core, mine, other, step):
    for at in range(0, value.shape[1] // unit, 2):
        even = value[:, at * unit : (at + 1) * unit]
        odd = value[:, (at + 1) * unit : (at + 2) * unit]
        cols = slice(at // 2 * unit, (at // 2 + 1) * unit)
        mine[step, :, cols] = jnp.where(core == 0, even, odd)
        other[step, :, cols] = jnp.where(core == 0, odd, even)


GELU_A = math.sqrt(2.0 / math.pi)
GELU_B = 0.044715


MESH_AXES = ("dp", "seq")


def axis_bits(dp_count, count):
    bits = []
    for axis, size in (("dp", dp_count), ("seq", count)):
        mask = size // 2
        while mask:
            bits.append((axis, mask))
            mask //= 2
    return bits


def stream_orders(dp_count, count):
    dp_bits = dp_count.bit_length() - 1
    seq_bits = count.bit_length() - 1
    dp_dims = list(range(dp_bits))
    seq_dims = list(range(dp_bits, dp_bits + seq_bits))[::-1]
    return (
        dp_dims[::-1] + seq_dims,
        dp_dims + seq_dims,
        seq_dims[:1] + dp_dims + seq_dims[1:],
        seq_dims[:1] + dp_dims[::-1] + seq_dims[1:],
    )


def my_bit(axis, mask):
    return lax.rem(lax.div(lax.axis_index(axis), mask), 2)


def partner(axis, mask):
    return lax.axis_index(axis) + mask * (1 - 2 * my_bit(axis, mask))


def greet(bits):
    barrier = pltpu.get_barrier_semaphore()
    for axis, mask in bits:
        pl.semaphore_signal(
            barrier,
            inc=1,
            device_id={axis: partner(axis, mask)},
            device_id_type=pl.DeviceIdType.MESH,
        )
    pl.semaphore_wait(barrier, len(bits))


class Reducer:
    def __init__(self, bits, order, src, cols, out, rows, compact, buffers, sems):
        self.bits, self.order, self.src, self.cols = bits, order, src, cols
        self.out, self.out_cols, self.buffers, self.sems = out, cols, buffers, sems
        self.count, self.rows, self.compact = len(bits), rows, compact

    @staticmethod
    def scratch(count, rows, width, dtype):
        shapes = [pltpu.VMEM((2,) * (count - 1) + (rows, width), dtype)]
        for stage in range(count):
            shapes.append(pltpu.VMEM((2,) * (count - 1 - stage) + (rows, width), dtype))
        shapes += [
            pltpu.SemaphoreType.DMA((count + 2,)),
            pltpu.SemaphoreType.DMA((count + 2,)),
            pltpu.SemaphoreType.DMA,
        ]
        return shapes

    def place(self, stage):
        left = [d for d in range(self.count) if d not in self.order[:stage]]
        dim = self.order[stage]
        return left, left.index(dim), self.bits[dim]

    def cut(self, stage, index):
        left, at, _ = self.place(stage)
        where = [slice(None)] * len(left)
        where[at] = index
        return tuple(where)

    def source(self, stage):
        if stage == 0:
            return self.src
        return self.buffers[0] if stage == 1 else self.buffers[stage]

    def copy(self, stage):
        axis, mask = self.place(stage)[2]
        where = self.cut(stage, 1 - my_bit(axis, mask))
        if stage == 0:
            where = where + (slice(None), pl.ds(*self.cols))
        return pltpu.make_async_remote_copy(
            src_ref=self.source(stage).at[where],
            dst_ref=self.buffers[stage + 1],
            send_sem=self.sems[0].at[stage],
            recv_sem=self.sems[1].at[stage],
            device_id={axis: partner(axis, mask)},
            device_id_type=pl.DeviceIdType.MESH,
        )

    def load(self):
        axis, mask = self.place(0)[2]
        where = self.cut(0, my_bit(axis, mask)) + (slice(None), pl.ds(*self.cols))
        return pltpu.make_async_copy(self.src.at[where], self.buffers[0], self.sems[2])

    def share(self):
        core = lax.axis_index("section")
        return pltpu.make_async_remote_copy(
            src_ref=self.out.at[core, :, pl.ds(*self.out_cols)],
            dst_ref=self.out.at[core, :, pl.ds(*self.out_cols)],
            send_sem=self.sems[0].at[self.count],
            recv_sem=self.sems[1].at[self.count],
            device_id={"section": 1 - core},
            device_id_type=pl.DeviceIdType.MESH,
        )

    def trade(self):
        third = self.rows // 3
        core = lax.axis_index("section")
        bit = lax.rem(lax.axis_index("seq"), 2)
        row = pl.multiple_of((1 - bit) * 2 * third, third)
        return pltpu.make_async_remote_copy(
            src_ref=self.out.at[core, pl.ds(row, third), pl.ds(*self.out_cols)],
            dst_ref=self.out.at[core, pl.ds(self.rows, third), pl.ds(*self.out_cols)],
            send_sem=self.sems[0].at[self.count + 1],
            recv_sem=self.sems[1].at[self.count + 1],
            device_id={"seq": partner("seq", 1)},
            device_id_type=pl.DeviceIdType.MESH,
        )

    def begin(self):
        self.copy(0).start()
        self.load().start()

    def step(self, stage):
        left, at, (axis, mask) = self.place(stage)
        bit = my_bit(axis, mask)
        if stage == 0:
            self.load().wait()
        self.copy(stage).wait_recv()
        got = self.buffers[stage + 1]
        rows = got.shape[-2]
        chunk = rows
        while chunk * got.shape[-1] > 65536 and chunk % 32 == 0:
            chunk //= 2
        per = rows // chunk
        last = stage == self.count - 1
        core = lax.axis_index("section")
        total = 2 ** (len(left) - 1)

        def body(i, carry):
            flat = lax.div(i, per)
            row = pl.multiple_of(lax.rem(i, per) * chunk, chunk)
            index = []
            for j in range(len(left) - 1):
                index.append(lax.rem(lax.div(flat, 2 ** (len(left) - 2 - j)), 2))
            there = tuple(index) + (pl.ds(row, chunk), slice(None))
            if stage == 0:
                mine = self.buffers[0][there]
            else:
                own = index[:at] + [bit] + index[at:]
                mine = self.source(stage)[tuple(own) + (pl.ds(row, chunk), slice(None))]
            value = mine.astype(F32) + got[there].astype(F32)
            if last:
                self.out[core, pl.ds(row, chunk), pl.ds(*self.out_cols)] = value
            elif stage == 0:
                self.buffers[0][there] = value.astype(got.dtype)
            else:
                got[there] = value.astype(got.dtype)
            return carry

        lax.fori_loop(0, total * per, body, 0)
        if not last:
            self.copy(stage + 1).start()
        elif self.compact:
            self.trade().start()
        else:
            self.share().start()

    def tail(self):
        if self.compact:
            self.trade().wait()
            self.share().start()

    def finish(self):
        for stage in range(self.count):
            self.copy(stage).wait_send()
        self.share().wait()


def part_widths(width):
    unit = 128 if width % 128 == 0 else width
    tiles = width // unit
    rest = tiles // 8
    first = -(-(tiles - rest) // 2)
    second = rest // 2
    return tuple(unit * n for n in (first, tiles - rest - first, rest - second, second))


STAGE_SHARES = (0.45, 0.7, 0.9, 1.0)


class Hosted:
    def __init__(self, dp_count, count, shapes, spans=None, shares=STAGE_SHARES, even=False):
        self.dp_count, self.count, self.shapes = dp_count, count, shapes
        self.spans = spans or ((0, 0.0, 1.0),) * len(shapes)
        self.all_bits = axis_bits(dp_count, count)
        self.plan = []
        for index, (rows, width, compact, _) in enumerate(shapes):
            bits = self.all_bits[:-1] if compact else self.all_bits
            orders = stream_orders(dp_count, count)
            widths = part_widths(width)
            if even and width % 256 == 0:
                widths = (width // 2, width // 2, 0, 0)
            if compact:
                last = len(bits)
                orders = [tuple(d for d in order if d != last) for order in orders[:2]]
                widths = (width // 2, width // 2)
            start = 0
            for order, size in zip(orders, widths):
                pieces = [size] if size else []
                if size >= 256 and not compact:
                    first = 128 * -(-size // 256)
                    pieces = [first, size - first]
                for k, piece in enumerate(pieces):
                    self.plan.append((index, tuple(order), bits, start, piece, rows, compact, k))
                    start += piece
        self.plan.sort(key=lambda p: (p[0], p[7]))
        self.arrays = len(shapes)
        self.events = []
        for k, part in enumerate(self.plan):
            phase, first, last = self.spans[part[0]]
            if phase == 0 and first > 0.0:
                self.events.append((first, k, -1))
            for stage in range(len(part[2])):
                share = shares[min(stage, 3)]
                self.events.append((first + (last - first) * share + 0.01 * stage, k, stage))
        self.events.sort()

    def views(self, arrays):
        return [self.view(i, array) for i, array in enumerate(arrays)]

    def view_shape(self, index):
        rows, width, compact, _ = self.shapes[index]
        depth = len(self.all_bits) - (1 if compact else 0)
        return (2,) * depth + (rows, width)

    def view(self, index, array):
        return array.reshape(self.view_shape(index))

    def in_specs(self):
        return [pl.BlockSpec(memory_space=pl.ANY)] * self.arrays

    def out_shapes(self):
        return [
            jax.ShapeDtypeStruct((2, rows + (rows // 3 if compact else 0), width), F32)
            for rows, width, compact, _ in self.shapes
        ]

    def out_specs(self):
        return [pl.BlockSpec(memory_space=pl.ANY)] * self.arrays

    def scratch(self):
        shapes = [pltpu.VMEM(o.shape, F32) for o in self.out_shapes()]
        shapes.append(pltpu.SemaphoreType.DMA((max(1, self.arrays),)))
        for index, _, bits, _, size, rows, _, _ in self.plan:
            shapes += Reducer.scratch(len(bits), rows, size, self.shapes[index][3])
        return shapes

    def bind(self, srcs, outs, scratch):
        self.parts = []
        self.outs, self.sums = outs, scratch[: self.arrays]
        self.out_sems = scratch[self.arrays]
        at = self.arrays + 1
        for index, order, bits, start, size, rows, compact, _ in self.plan:
            depth = len(bits) + 1
            mine = scratch[at : at + depth + 3]
            at += depth + 3
            self.parts.append(
                Reducer(
                    bits,
                    order,
                    srcs[index],
                    (start, size),
                    self.sums[index],
                    rows,
                    compact,
                    mine[:depth],
                    mine[depth:],
                )
            )

    def begin(self, phase=0):
        for part, plan in zip(self.parts, self.plan):
            span = self.spans[plan[0]]
            if span[0] == phase and (phase or span[1] == 0.0):
                part.begin()

    def run(self, first, last):
        for _, k, stage in self.events[first:last]:
            if stage < 0:
                self.parts[k].begin()
            else:
                self.parts[k].step(stage)

    def slots(self, times):
        edges = []
        done = 0
        for time in times:
            while done < len(self.events) and self.events[done][0] <= time:
                done += 1
            edges.append(done)
        edges[-1] = len(self.events)
        return list(zip([0] + edges[:-1], edges))

    def settle(self):
        for part in self.parts:
            part.tail()
        for part in self.parts:
            part.finish()

    def finish(self):
        self.settle()
        copies = []
        for i, (out, value) in enumerate(zip(self.outs, self.sums)):
            copies.append(pltpu.make_async_copy(value, out, self.out_sems.at[i]))
            copies[-1].start()
        for copy in copies:
            copy.wait()


BACK_LIMIT = 64 * 2**20 - 2**18


class Group:
    def __init__(self):
        self.half = lax.axis_size("seq") // 2
        self.core = lax.axis_index("section")
        self.place = lax.axis_index("seq")
        self.low = lax.rem(self.place, self.half)
        self.base = self.place - self.low
        self.rank = self.core * self.half + self.low

    def others(self):
        pairs = [(dc, d) for d in range(1, self.half) for dc in (0, 1)]
        return pairs + [(1, 0)]

    def slot(self, dc, d):
        return dc * self.half + d

    def where(self, dc, d):
        core = lax.rem(self.core + dc, 2)
        low = lax.rem(self.low + d, self.half)
        return core, low

    def device(self, dc, d):
        core, low = self.where(dc, d)
        return {"section": core, "seq": self.base + low}

    def rank_of(self, dc, d):
        core, low = self.where(dc, d)
        return core * self.half + low

    def greet(self, dp_count):
        barrier = pltpu.get_barrier_semaphore()
        targets = [self.device(dc, d) for dc, d in self.others()]
        mask = dp_count // 2
        while mask:
            targets.append({"dp": partner("dp", mask)})
            mask //= 2
        targets.append({"seq": partner("seq", self.half)})
        targets.append({"section": 1 - self.core, "seq": partner("seq", self.half)})
        for target in targets:
            pl.semaphore_signal(
                barrier, inc=1, device_id=target, device_id_type=pl.DeviceIdType.MESH
            )
        pl.semaphore_wait(barrier, len(targets))


def send(src, dst, sems, slot, device):
    return pltpu.make_async_remote_copy(
        src_ref=src,
        dst_ref=dst,
        send_sem=sems[0].at[slot],
        recv_sem=sems[1].at[slot],
        device_id=device,
        device_id_type=pl.DeviceIdType.MESH,
    )


class Deliver:
    def __init__(self, group, layer, src, out, sems):
        micro = lax.div(group.place, group.half)
        here, there = sems[0], sems[1]
        self.core, self.layer = group.core, layer
        self.local = pltpu.make_async_copy(src, out.at[micro], sems[2])
        self.chip = send(src, out.at[micro], (here, there), 0, {"section": 1 - group.core})
        self.far = send(
            src,
            out.at[micro],
            (here, there),
            1,
            {"section": layer, "seq": partner("seq", group.half)},
        )

    def start(self):
        first = self.local if self.layer == 0 else self.chip
        pl.when(self.core == 0)(lambda: first.start())
        pl.when(self.core == 1)(lambda: self.far.start())

    def wait(self):
        @pl.when(self.core == 0)
        def _():
            if self.layer == 0:
                self.local.wait()
                self.far.wait_recv()
            else:
                self.chip.wait_send()

        @pl.when(self.core == 1)
        def _():
            self.far.wait_send()
            if self.layer == 1:
                self.far.wait_recv()
                self.chip.wait_recv()


def deliver_sems():
    return dma_pair(2) + [pltpu.SemaphoreType.DMA]


def dma_pair(count):
    return [pltpu.SemaphoreType.DMA((count,)), pltpu.SemaphoreType.DMA((count,))]


VEC_ROWS = 16
LN1_GAIN, LN1_BIAS, B_QUERY, B_VALUE, B_OUT, LN2_GAIN, LN2_BIAS, B_DOWN, B_UP = range(9)


def attend_kernel(first, layer, dp_count, *refs):
    if first:
        x_ref, joint_ref, wout_ref, mask_ref = refs[:4]
        vectors = refs[4:13]
        o_out, lse_out, a_out, q_out, k_out, v_out = refs[13:19]
        x_out, joint_out, wout_out, vec_out = refs[19:23]
        rest = refs[23:]
    else:
        x_ref, joint_ref, mask_ref, vec_ref, cot_ref = refs[:5]
        o_out, lse_out, a_out, q_out, k_out, v_out, cot_out = refs[5:12]
        rest = refs[12:]
    x_all, a_all, q_all, k_all, v_all, lse, o_send, o_recv = rest[:8]
    x_sems, o_sems = rest[8:10], rest[10:12]
    out_sems = rest[12]
    if first:
        joint_pair, wide_own, wide_other, vec_send, vec_recv, vec_pair = rest[13:19]
        wide_sems, vec_sems = rest[19:21], rest[21:23]
        load_sems = rest[23]
    else:
        joint_one, cot_own, cot_other = rest[13:16]
        cot_sems = rest[16:18]
        load_sems = rest[18]
    group = Group()
    core, half, rank, low = group.core, group.half, group.rank, group.low
    ranks, rows, _ = x_all.shape
    width = q_all.shape[1]
    heads = width // DH
    span = half * width
    partner_core = group.device(1, 0)
    micro = lax.div(group.place, half)

    group.greet(dp_count)

    def x_copy(slot, from_rank, device):
        return send(x_all.at[from_rank], x_all.at[from_rank], x_sems, slot, device)

    far = {"seq": partner("seq", half)}

    if first:
        own_load = pltpu.make_async_copy(x_ref.at[micro, 0], x_all.at[rank], load_sems.at[0])
        far_copy = send(x_ref.at[1 - micro, 0], x_all.at[rank], x_sems, 2 * half - 1, far)
        pl.when(core == 1)(lambda: far_copy.start())
        pl.when(core == 0)(lambda: own_load.start())
        wide_copies = []
        own_loads = []
        for part in range(3):
            theirs = pl.ds(pl.multiple_of(part * D + (1 - core) * span, 128), span)
            ours = pl.ds(pl.multiple_of(part * D + core * span, 128), span)
            wide_copies.append(
                send(joint_ref.at[0, :, theirs], wide_other.at[part], wide_sems, part, partner_core)
            )
            own_loads.append(
                pltpu.make_async_copy(
                    joint_ref.at[0, :, ours], wide_own.at[part], load_sems.at[1 + part]
                )
            )
            wide_copies[-1].start()
            own_loads[-1].start()
        vec_send[...] = jnp.zeros_like(vec_send)
        for i, value in enumerate(vectors[:8]):
            vec_send[i : i + 1, :] = value[...].astype(F32)
        for i in range(FF // D):
            vec_send[8 + i : 9 + i, :] = vectors[8][:, i * D : (i + 1) * D].astype(F32)
        vec_copy = send(vec_send, vec_recv, vec_sems, 0, partner_core)
        vec_copy.start()
        wout_copy = send(wout_ref.at[0], wout_out, vec_sems, 1, partner_core)
        pl.when(core == 1)(lambda: far_copy.wait_recv())
        pl.when(core == 0)(lambda: own_load.wait())
    else:
        own_load = pltpu.make_async_copy(x_ref, x_all.at[rank], load_sems.at[0])
        joint_load = pltpu.make_async_copy(joint_ref.at[1], joint_one, load_sems.at[1])
        own_load.start()
        joint_load.start()
        cot_far = send(cot_ref.at[1 - micro, 0], cot_own, cot_sems, 0, far)
        cot_load = pltpu.make_async_copy(cot_ref.at[micro, 0], cot_own, load_sems.at[2])
        pl.when(core == 1)(lambda: cot_far.start())
        pl.when(core == 0)(lambda: cot_load.start())
        own_load.wait()
    for d in range(1, half):
        x_copy(d - 1, rank, group.device(0, d)).start()
    x_copy(half - 1, rank, partner_core).start()

    source = lax.broadcasted_iota(jnp.int32, (span, width), 0)
    target = lax.broadcasted_iota(jnp.int32, (span, width), 1)
    if half == 2:
        wanted = (2 * lax.div(target, DH) + low) * DH + lax.rem(target, DH)
    else:
        wanted = low * width + target
    pick = (source == wanted).astype(F32).astype(BF16)
    if first:
        wout_copy.start()
        vec_copy.wait_recv()
        vec_pair[core] = vec_send[...]
        vec_pair[1 - core] = vec_recv[...]
        for load in own_loads:
            load.wait()
        for part in range(3):
            joint_pair[core, :, part * width : (part + 1) * width] = mm(
                wide_own[part], pick
            ).astype(BF16)
        for copy in wide_copies:
            copy.wait_recv()
        for part in range(3):
            joint_pair[1 - core, :, part * width : (part + 1) * width] = mm(
                wide_other[part], pick
            ).astype(BF16)
        vec = vec_pair[0]
        weights = lambda: joint_pair[0]
    else:
        joint_load.wait()
        vec = vec_ref[1]
        weights = lambda: joint_one[...]

    def of_heads(row):
        parts = vec[row : row + 1, :]
        mine = jnp.where(core == 0, parts[:, :span], parts[:, span:])
        wide = jnp.broadcast_to(mine, (16, span)).astype(BF16)
        return mm(wide, pick)[0:1, :]

    bias_q = of_heads(B_QUERY)
    bias_v = of_heads(B_VALUE)
    gain = vec[LN1_GAIN : LN1_GAIN + 1, :]
    shift = vec[LN1_BIAS : LN1_BIAS + 1, :]

    def project(at):
        normal, _ = norm_stats(x_all[at].astype(F32))
        a = (normal * gain + shift).astype(BF16)
        here = pl.ds(pl.multiple_of(at * rows, 16), rows)
        a_all[here, :] = a
        joined = mm(a, weights())
        q_all[here, :] = (joined[:, :width] + bias_q).astype(BF16)
        k_all[here, :] = joined[:, width : 2 * width].astype(BF16)
        v_all[here, :] = (joined[:, 2 * width :] + bias_v).astype(BF16)

    project(rank)
    x_copy(half - 1, rank, partner_core).wait_recv()
    project(group.rank_of(1, 0))
    for d in range(1, half):
        here = group.rank_of(0, half - d)
        x_copy(d - 1, here, partner_core).wait_recv()
        x_copy(half - 1 + d, here, partner_core).start()
        project(here)
    for d in range(1, half):
        there = group.rank_of(1, half - d)
        x_copy(half - 1 + d, there, partner_core).wait_recv()
        project(there)

    saves = [
        pltpu.make_async_copy(a_all, a_out, out_sems.at[0]),
        pltpu.make_async_copy(q_all, q_out, out_sems.at[1]),
        pltpu.make_async_copy(k_all, k_out, out_sems.at[2]),
        pltpu.make_async_copy(v_all, v_out, out_sems.at[3]),
    ]
    if first:
        saves.append(pltpu.make_async_copy(joint_pair, joint_out, out_sems.at[4]))
        saves.append(pltpu.make_async_copy(x_all.at[rank], x_out, out_sems.at[5]))
        saves.append(pltpu.make_async_copy(vec_pair, vec_out, out_sems.at[6]))
    for save in saves:
        save.start()
    lane = lax.broadcasted_iota(jnp.int32, (rows, 128), 1)
    mask = mask_ref[...]

    def attend(at):
        here = pl.ds(pl.multiple_of(at * rows, 16), rows)
        q = q_all[here, :]
        mixed = jnp.zeros((rows, width), F32)
        totals = jnp.zeros((rows, 128), F32)
        for head in range(heads):
            mine = head_lanes((rows, width), head)
            scores = mm_nt(jnp.where(mine, q, jnp.zeros_like(q)), k_all[...]) * SCALE2 + mask
            top = jnp.max(scores, axis=-1, keepdims=True)
            expo = jnp.exp2(scores - top)
            total = jnp.sum(expo, axis=-1, keepdims=True)
            part = mm(expo.astype(BF16), v_all[...]) / total
            mixed = jnp.where(mine, part, mixed)
            totals = jnp.where(lane == head, top + jnp.log2(total), totals)
        lse[here, :] = totals
        return mixed.astype(BF16)

    copies = []
    for dc, d in group.others():
        slot = group.slot(dc, d)
        o_send[slot] = attend(group.rank_of(dc, d))
        copies.append(send(o_send.at[slot], o_recv.at[rank], o_sems, slot, group.device(dc, d)))
        copies[-1].start()
    if not first:
        pl.when(core == 1)(lambda: cot_far.wait())
        pl.when(core == 0)(lambda: cot_load.wait())
        cot_share = send(cot_own, cot_other, cot_sems, 1, partner_core)
        cot_share.start()
    o_recv[rank] = attend(rank)
    if not first:
        cot_share.wait()
        cot_out[0] = cot_own[...]
        cot_out[1] = cot_other[...]
    lse_out[...] = lse[...]
    for copy in copies:
        copy.wait()
    o_out[...] = o_recv[...]
    for save in saves:
        save.wait()
    for d in range(1, half):
        x_copy(d - 1, rank, group.device(0, d)).wait_send()
        x_copy(half - 1 + d, group.rank_of(0, half - d), partner_core).wait_send()
    x_copy(half - 1, rank, partner_core).wait_send()
    if first:
        pl.when(core == 1)(lambda: far_copy.wait_send())
        for copy in wide_copies:
            copy.wait_send()
        vec_copy.wait_send()
        wout_copy.wait()


def attend_call(first, layer, mask, ranks, dp_count, *args):
    rows = args[0].shape[-2]
    width = D // ranks
    half = ranks // 2
    span = half * width
    anywhere = pl.BlockSpec(memory_space=pl.ANY)
    vmem = pl.BlockSpec(memory_space=pltpu.VMEM)
    out_shape = [
        jax.ShapeDtypeStruct((ranks, rows, width), BF16),
        jax.ShapeDtypeStruct((LEN, 128), F32),
        jax.ShapeDtypeStruct((LEN, D), BF16),
        jax.ShapeDtypeStruct((LEN, width), BF16),
        jax.ShapeDtypeStruct((LEN, width), BF16),
        jax.ShapeDtypeStruct((LEN, width), BF16),
    ]
    out_specs = [vmem, vmem] + [anywhere] * 4
    scratch = [
        pltpu.VMEM((ranks, rows, D), BF16),
        pltpu.VMEM((LEN, D), BF16),
        pltpu.VMEM((LEN, width), BF16),
        pltpu.VMEM((LEN, width), BF16),
        pltpu.VMEM((LEN, width), BF16),
        pltpu.VMEM((LEN, 128), F32),
        pltpu.VMEM((ranks, rows, width), BF16),
        pltpu.VMEM((ranks, rows, width), BF16),
    ]
    scratch += dma_pair(2 * half) + dma_pair(ranks) + [pltpu.SemaphoreType.DMA((7,))]
    if first:
        operands = args[:3] + (mask,) + args[3:]
        in_specs = [anywhere] * 3 + [vmem] * (1 + len(args[3:]))
        out_shape += [
            jax.ShapeDtypeStruct((rows, D), BF16),
            jax.ShapeDtypeStruct((2, D, 3 * width), BF16),
            jax.ShapeDtypeStruct((D, D), BF16),
            jax.ShapeDtypeStruct((2, VEC_ROWS, D), F32),
        ]
        out_specs += [anywhere] * 4
        scratch += [
            pltpu.VMEM((2, D, 3 * width), BF16),
            pltpu.VMEM((3, D, span), BF16),
            pltpu.VMEM((3, D, span), BF16),
            pltpu.VMEM((VEC_ROWS, D), F32),
            pltpu.VMEM((VEC_ROWS, D), F32),
            pltpu.VMEM((2, VEC_ROWS, D), F32),
        ]
        scratch += dma_pair(3) + dma_pair(2) + [pltpu.SemaphoreType.DMA((4,))]
    else:
        operands = args[:2] + (mask,) + args[2:]
        in_specs = [anywhere] * 2 + [vmem] * 2 + [anywhere]
        out_shape += [jax.ShapeDtypeStruct((2, rows, D), BF16)]
        out_specs += [vmem]
        scratch += [
            pltpu.VMEM((D, 3 * width), BF16),
            pltpu.VMEM((rows, D), BF16),
            pltpu.VMEM((rows, D), BF16),
        ]
        scratch += dma_pair(2) + [pltpu.SemaphoreType.DMA((3,))]
    return pl.pallas_call(
        functools.partial(attend_kernel, first, layer, dp_count),
        in_specs=in_specs,
        out_specs=out_specs,
        out_shape=out_shape,
        scratch_shapes=scratch,
        compiler_params=pltpu.CompilerParams(
            vmem_limit_bytes=VMEM_LIMIT, collective_id=5 + layer, has_side_effects=True
        ),
        cost_estimate=pl.CostEstimate(
            flops=40 * 10**9, bytes_accessed=20 * 2**20, transcendentals=LEN * LEN * width // DH
        ),
    )(*operands)


def mlp_kernel(
    layer,
    dp_count,
    o_ref,
    x_ref,
    wo0_ref,
    wo1_ref,
    vec_ref,
    up0_ref,
    up1_ref,
    down0_ref,
    down1_ref,
    h_ref,
    u_ref,
    y_ref,
    a_all,
    o_all,
    g_all,
    rows_out,
    acc,
    wo,
    a_mine,
    a_other,
    o_send,
    o_other,
    g_mine,
    g_send,
    g_other,
    send_sems,
    recv_sems,
    save_sems,
    wo_sem,
    rows_mine,
    *rows_sems,
):
    step = pl.program_id(0)
    groups, rows, width = o_ref.shape
    half = groups // 2
    unit = FF // shards_of() // 2
    core = lax.axis_index("section")
    own = core == layer
    device = {"section": 1 - core}
    sems = (send_sems, recv_sems)
    if layer == 1:
        rows_copy = Deliver(Group(), 0, rows_mine, rows_out, rows_sems)
    a_copy = send(a_mine, a_other, sems, NCHF, device)
    o_copy = send(o_send, o_other, sems, NCHF + 1, device)

    def g_copy(at):
        return send(g_send.at[at], g_other.at[at], sems, at, device)

    def g_save(which, at):
        cols = pl.ds(pl.multiple_of(at * (FCF // 2), FCF // 2), FCF // 2)
        source = g_other if which else g_mine
        return pltpu.make_async_copy(
            source.at[at], g_all.at[which, :, cols], save_sems.at[which, at]
        )

    @pl.when(step == 0)
    def _():
        Group().greet(dp_count)
        if layer == 1:
            rows_mine[...] = x_ref[...]
            rows_copy.start()
        first = pltpu.make_async_copy(wo0_ref, wo, wo_sem)
        second = pltpu.make_async_copy(wo1_ref, wo, wo_sem)
        pl.when(own)(lambda: first.start())
        pl.when(jnp.logical_not(own))(lambda: second.start())
        for i in range(half):
            o_send[i] = o_ref[(1 - core) * half + i]
            o_all[0, :, i * width : (i + 1) * width] = o_ref[core * half + i]
        o_copy.start()
        first.wait()
        hidden = x_ref[...].astype(F32) + vec_ref[0, B_OUT : B_OUT + 1, :]
        for group in range(groups):
            hidden += mm(o_ref[group], wo[group * width : (group + 1) * width, :])
        h_ref[...] = hidden
        normal, _ = norm_stats(hidden)
        a_mine[...] = (
            normal * vec_ref[0, LN2_GAIN : LN2_GAIN + 1, :] + vec_ref[0, LN2_BIAS : LN2_BIAS + 1, :]
        ).astype(BF16)
        a_copy.start()
        acc[...] = hidden + vec_ref[0, B_DOWN : B_DOWN + 1, :]

    def part(up_ref, down_ref):
        at = pl.multiple_of(lax.rem(step, D // FCF) * FCF, FCF)
        bias = vec_ref[0, pl.ds(B_UP + lax.div(step, D // FCF), 1), pl.ds(at, FCF)]
        upper = mm(a_mine[...], up_ref[...]) + bias
        u_ref[...] = upper
        inner = GELU_A * (upper + GELU_B * upper * upper * upper)
        gated = (0.5 * upper * (1.0 + jnp.tanh(inner))).astype(BF16)
        split_halves(gated, unit, core, g_mine, g_send, step)
        acc[...] += mm(gated, down_ref[...])

    @pl.when(step < NCHF)
    def _():
        pl.when(own)(lambda: part(up0_ref, down0_ref))
        pl.when(jnp.logical_not(own))(lambda: part(up1_ref, down1_ref))
        g_copy(step).start()
        g_save(0, step).start()

    @pl.when(step > 0)
    def _():
        g_copy(step - 1).wait()
        g_save(1, step - 1).start()

    @pl.when(step == NCHF)
    def _():
        y_ref[...] = acc[...].astype(BF16)
        a_copy.wait()
        a_all[0] = a_mine[...]
        a_all[1] = a_other[...]
        o_copy.wait()
        for i in range(half):
            o_all[1, :, i * width : (i + 1) * width] = o_other[i]

        def drain(at, carry):
            g_save(0, at).wait()
            g_save(1, at).wait()
            return carry

        lax.fori_loop(0, NCHF, drain, 0)
        if layer == 1:
            rows_copy.wait()


def mlp_call(layer, dp_count, o_all, x_own, outs, vec, ups, downs):
    rows = x_own.shape[0]
    groups, _, width = o_all.shape
    whole = lambda i: (0, 0)
    now = lambda i: jnp.minimum(i, NCHF - 1)
    mine = lambda i, first: jnp.where((lax.axis_index("section") == layer) == first, now(i), 0)
    col = lambda first: (lambda i: (0, mine(i, first)))
    line = lambda first: (lambda i: (mine(i, first), 0))
    chunk = lambda i: (0, now(i))
    piece = pltpu.VMEM((NCHF, rows, FCF // 2), BF16)
    return pl.pallas_call(
        functools.partial(mlp_kernel, layer, dp_count),
        grid=(NCHF + 1,),
        in_specs=[
            pl.BlockSpec((groups, rows, width), lambda i: (0, 0, 0)),
            pl.BlockSpec((rows, D), whole),
            pl.BlockSpec(memory_space=pl.ANY),
            pl.BlockSpec(memory_space=pl.ANY),
            pl.BlockSpec((1, VEC_ROWS, D), lambda i: (layer, 0, 0)),
            pl.BlockSpec((D, FCF), col(True)),
            pl.BlockSpec((D, FCF), col(False)),
            pl.BlockSpec((FCF, D), line(True)),
            pl.BlockSpec((FCF, D), line(False)),
        ],
        out_specs=[
            pl.BlockSpec((rows, D), whole),
            pl.BlockSpec((rows, FCF), chunk),
            pl.BlockSpec((rows, D), whole),
            pl.BlockSpec((2, rows, D), lambda i: (0, 0, 0)),
            pl.BlockSpec((2, rows, D // 2), lambda i: (0, 0, 0)),
            pl.BlockSpec(memory_space=pl.ANY),
            pl.BlockSpec(memory_space=pl.ANY),
        ],
        scratch_shapes=[
            pltpu.VMEM((rows, D), F32),
            pltpu.VMEM((D, D), BF16),
            pltpu.VMEM((rows, D), BF16),
            pltpu.VMEM((rows, D), BF16),
            pltpu.VMEM((groups // 2, rows, width), BF16),
            pltpu.VMEM((groups // 2, rows, width), BF16),
            piece,
            piece,
            piece,
        ]
        + dma_pair(NCHF + 2)
        + [pltpu.SemaphoreType.DMA((2, NCHF)), pltpu.SemaphoreType.DMA]
        + [pltpu.VMEM((rows, D), BF16)]
        + deliver_sems(),
        out_shape=[
            jax.ShapeDtypeStruct((rows, D), F32),
            jax.ShapeDtypeStruct((rows, FF), F32),
            jax.ShapeDtypeStruct((rows, D), BF16),
            jax.ShapeDtypeStruct((2, rows, D), BF16),
            jax.ShapeDtypeStruct((2, rows, D // 2), BF16),
            jax.ShapeDtypeStruct((2, rows, FF // 2), BF16),
            jax.ShapeDtypeStruct((2, rows, D), BF16),
        ],
        compiler_params=pltpu.CompilerParams(
            vmem_limit_bytes=VMEM_LIMIT, collective_id=7 + layer, has_side_effects=True
        ),
        cost_estimate=pl.CostEstimate(
            flops=2 * rows * D * (D + 2 * FF), bytes_accessed=30 * 2**20, transcendentals=rows * FF
        ),
    )(o_all, x_own, outs[0], outs[1], vec, ups[0], ups[1], downs[0], downs[1])


def back_kernel(layer, host, ranges, *refs):
    n = host.arrays - 1
    refs = list(refs)

    def pop(count):
        taken = refs[:count]
        del refs[:count]
        return taken

    u_ref, mask_ref, vec_ref = pop(3)
    dy_src, h_src, a2_src, wo0_src, wo1_src, up0_src, up1_src, down0_src, down1_src = pop(9)
    rows_src = pop(1)[0]
    late = pop(8)
    srcs = pop(n)
    gbup_ref, sums_two_ref, sums_one_ref, sums_qv_ref = pop(4)
    gup_out, dx_out, gjoint_out, gout_out, rows_out = pop(5)
    outs = pop(n + 1)
    dy, h, a2, wo, ups, downs = pop(6)
    load_sems, weight_sems = pop(2)
    acc, du_mine, du_send, du_recv, gup, branch, dh, do_send, do_recv = pop(9)
    du_sems, do_sems = pop(2), pop(2)
    gup_sems, save_sems = pop(2)
    q_all, k_all, v_all, lse, a1, w_joint, x_own, mixed = pop(8)
    late_sems = pop(1)[0]
    dk_acc, dv_acc, dj, core_recv, far_send, far_recv = pop(6)
    core_send = a2 if lax.axis_size("seq") == 4 else pop(1)[0]
    g_own, g_send, g_recv, gout, dx_recv = pop(5)
    dx_own = dy
    core_sems, far_sems, pair_sems = pop(2), pop(2), pop(2)
    rows_sems = pop(3)
    host.bind(list(srcs) + [gup_out], outs, refs)
    group = Group()
    core, half, rank = group.core, group.half, group.rank
    step = pl.program_id(0)
    ranks, rows, width = do_send.shape
    length = q_all.shape[0]
    heads = width // DH
    scale = DH ** (-0.5)
    unit = FF // shards_of() // 2
    own = core == layer
    partner_core = group.device(1, 0)
    ranges = list(ranges)
    lead, middle = ranges[: 2 * NCH], ranges[2 * NCH : 2 * NCH + 3]
    blocks = length // BQ * heads
    inner = ranges[2 * NCH + 3 : 2 * NCH + 3 + blocks]
    tail = ranges[2 * NCH + 3 + blocks :]

    def weight_copies(at, second):
        slot = lax.rem(at, 2)
        cols = pl.ds(pl.multiple_of(at * FC, FC), FC)
        up, down = (up1_src, down1_src) if second else (up0_src, down0_src)
        return (
            pltpu.make_async_copy(up.at[:, cols], ups.at[slot], weight_sems.at[0, slot]),
            pltpu.make_async_copy(down.at[cols, :], downs.at[slot], weight_sems.at[1, slot]),
        )

    def fetch(at):
        @pl.when(own)
        def _():
            for copy in weight_copies(at, False):
                copy.start()

        @pl.when(jnp.logical_not(own))
        def _():
            for copy in weight_copies(at, True):
                copy.start()

    rows_copy = Deliver(group, 1, rows_src.at[0], rows_out, rows_sems)
    dy_load = pltpu.make_async_copy(dy_src.at[0], dy, load_sems.at[0])
    h_load = pltpu.make_async_copy(h_src, h, load_sems.at[1])
    a2_load = pltpu.make_async_copy(a2_src, a2, load_sems.at[2])
    wo_load = pltpu.make_async_copy(wo0_src, wo, load_sems.at[3])
    wo_load_other = pltpu.make_async_copy(wo1_src, wo, load_sems.at[3])
    late_loads = [
        pltpu.make_async_copy(source.at[layer] if i == 5 else source, target, late_sems.at[i])
        for i, (source, target) in enumerate(
            zip(late, (q_all, k_all, v_all, lse, a1, w_joint, x_own, mixed))
        )
    ]

    def du_copy(at):
        return send(du_send.at[at], du_recv.at[at], du_sems, at, partner_core)

    def gup_save(at):
        per = gup.shape[1]
        lead_bits = NCH.bit_length() - 1
        index = tuple(
            lax.rem(lax.div(at, 2 ** (lead_bits - 1 - j)), 2) for j in range(lead_bits)
        )
        return pltpu.make_async_copy(
            gup.at[lax.rem(at, 2)].reshape(gup_out.shape[lead_bits:]),
            gup_out.at[index],
            gup_sems.at[lax.rem(at, 2)],
        )

    @pl.when(step == 0)
    def _():
        group.greet(host.dp_count)
        rows_copy.start()
        dy_load.start()
        fetch(0)
        host.begin()
        a2_load.start()
        h_load.start()
        pl.when(own)(lambda: wo_load.start())
        pl.when(jnp.logical_not(own))(lambda: wo_load_other.start())
        for load in late_loads:
            load.start()
        acc[...] = jnp.zeros_like(acc)
        dy_load.wait()
        a2_load.wait()

    @pl.when(step < NCH - 1)
    def _():
        fetch(step + 1)

    @pl.when(step < NCH)
    def _():
        slot = lax.rem(step, 2)
        for copy in weight_copies(step, False):
            copy.wait()
        d_gated = mm_nt(dy[...], downs[slot])
        upper = u_ref[...]
        square = upper * upper
        turn = jnp.tanh(GELU_A * upper * (1.0 + GELU_B * square))
        slope = 0.5 * (1.0 + turn) + (0.5 * GELU_A) * upper * (1.0 - turn * turn) * (
            1.0 + (3.0 * GELU_B) * square
        )
        d_upper = (d_gated * slope).astype(BF16)
        split_halves(d_upper, unit, core, du_mine, du_send, step)
        du_copy(step).start()
        gbup_ref[...] = jnp.sum(d_upper.astype(F32), axis=0, keepdims=True)
        acc[...] += mm_nt(d_upper, ups[slot])

    for at, (first, last) in enumerate(lead):
        if last > first and at % 2 == 0:
            pl.when(step == at // 2)(functools.partial(host.run, first, last))

    @pl.when(step > 0)
    def _():
        at = step - 1
        du_copy(at).wait()
        pl.when(at >= 2)(lambda: gup_save(at - 2).wait())
        value = mm_tn(du_mine[at], a2[0]) + mm_tn(du_recv[at], a2[1])
        gup[lax.rem(at, 2)] = value.astype(BF16).reshape(gup.shape[1:])
        gup_save(at).start()

    for at, (first, last) in enumerate(lead):
        if last > first and at % 2 == 1:
            pl.when(step == at // 2)(functools.partial(host.run, first, last))

    @pl.when(step == NCH)
    def _():
        h_load.wait()
        gup_save(NCH - 2).wait()
        gup_save(NCH - 1).wait()
        host.begin(1)
        normal, inverse = norm_stats(h[...])
        d_out = dy[...].astype(F32)
        d_normed = acc[...]
        sums_two_ref[...] = jnp.zeros_like(sums_two_ref)
        sums_two_ref[0:1, :] = jnp.sum(d_normed * normal, axis=0, keepdims=True)
        sums_two_ref[1:2, :] = jnp.sum(d_normed, axis=0, keepdims=True)
        d_normal = d_normed * vec_ref[0, LN2_GAIN : LN2_GAIN + 1, :]
        d_hidden = d_out + inverse * (
            d_normal
            - jnp.mean(d_normal, axis=-1, keepdims=True)
            - normal * jnp.mean(d_normal * normal, axis=-1, keepdims=True)
        )
        dh[...] = d_hidden
        d_branch = d_hidden.astype(BF16)
        branch[0] = d_branch
        branch_copy = send(branch.at[0], branch.at[1], do_sems, ranks, partner_core)
        branch_copy.start()
        wo_load.wait()

        def heads_of(to_rank):
            at = pl.multiple_of(to_rank * width, width)
            return mm_nt(d_branch, wo[pl.ds(at, width), :]).astype(BF16)

        copies = []
        for dc, d in group.others():
            slot = group.slot(dc, d)
            do_send[slot] = heads_of(group.rank_of(dc, d))
            copies.append(
                send(do_send.at[slot], do_recv.at[pl.ds(pl.multiple_of(rank * rows, 16), rows)], do_sems, slot, group.device(dc, d))
            )
            copies[-1].start()
        do_recv[pl.ds(pl.multiple_of(rank * rows, 16), rows), :] = heads_of(rank)
        host.run(*middle[0])
        sums_two_ref[2:3, :] = jnp.sum(d_branch.astype(F32), axis=0, keepdims=True)
        sums_two_ref[3:4, :] = jnp.sum(d_out, axis=0, keepdims=True)
        dk_acc[...] = jnp.zeros_like(dk_acc)
        dv_acc[...] = jnp.zeros_like(dv_acc)
        sums_qv_ref[...] = jnp.zeros_like(sums_qv_ref)
        sums_one_ref[...] = jnp.zeros_like(sums_one_ref)
        for load in late_loads:
            load.wait()
        branch_copy.wait()
        gout[...] = (mm_tn(branch[0], mixed[0]) + mm_tn(branch[1], mixed[1])).astype(BF16)
        gout_save = pltpu.make_async_copy(gout, gout_out, save_sems.at[0])
        gout_save.start()
        host.run(*middle[1])
        for copy in copies:
            copy.wait()
        host.run(*middle[2])

        def block(at, carry):
            here = pl.ds(pl.multiple_of(at * BQ, BQ), BQ)
            q = q_all[here, :]
            grad = do_recv[here, :]
            totals = lse[here, :]
            d_q = jnp.zeros((BQ, width), F32)
            for head in range(heads):
                mine = head_lanes((BQ, width), head)
                q_head = jnp.where(mine, q, jnp.zeros_like(q))
                grad_head = jnp.where(mine, grad, jnp.zeros_like(grad))
                scores = mm_nt(q_head, k_all[...]) * SCALE2 + mask_ref[...]
                probs = jnp.exp2(scores - totals[:, head : head + 1])
                d_probs = mm_nt(grad_head, v_all[...])
                term = jnp.sum(probs * d_probs, axis=-1, keepdims=True)
                d_scores = (probs * (d_probs - term)).astype(BF16)
                dv_acc[...] += mm_tn(probs.astype(BF16), grad_head)
                dk_acc[...] += mm_tn(d_scores, q_head)
                d_q = jnp.where(mine, mm(d_scores, k_all[...]), d_q)
                for slot, (first, last) in enumerate(inner):
                    if last > first and slot % heads == head:
                        pl.when(at == slot // heads)(functools.partial(host.run, first, last))
            low = (d_q * scale).astype(BF16)
            dj[here, :width] = low
            sums_qv_ref[0:1, :] += jnp.sum(low.astype(F32), axis=0, keepdims=True)
            return carry

        lax.fori_loop(0, length // BQ, block, 0)
        dj[:, width : 2 * width] = (dk_acc[...] * scale).astype(BF16)
        low_v = dv_acc[...].astype(BF16)
        dj[:, 2 * width :] = low_v
        sums_qv_ref[1:2, :] = jnp.sum(low_v.astype(F32), axis=0, keepdims=True)

        def partial_rows(to_rank):
            here = pl.ds(pl.multiple_of(to_rank * rows, 16), rows)
            return mm_nt(dj[here, :], w_joint[...])

        def core_copy(d):
            return send(core_send.at[d], core_recv.at[d], core_sems, d, partner_core)

        def far_copy(d):
            return send(far_send.at[d - 1], far_recv.at[d - 1], far_sems, d - 1, group.device(0, d))

        for d in [d for d in range(1, half)] + [0]:
            core_send[d] = partial_rows(group.rank_of(1, d)).astype(BF16)
            core_copy(d).start()
        for d in range(1, half):
            value = partial_rows(group.rank_of(0, d))
            core_copy(d).wait_recv()
            far_send[d - 1] = (value + core_recv[d].astype(F32)).astype(BF16)
            far_copy(d).start()
        host.run(*tail[0])
        value = partial_rows(rank)
        core_copy(0).wait_recv()
        acc[...] = value + core_recv[0].astype(F32)

        half_cols = D // 2
        mine_cols = pl.ds(pl.multiple_of(core * half_cols, half_cols), half_cols)
        other_cols = pl.ds(pl.multiple_of((1 - core) * half_cols, half_cols), half_cols)
        g_send[...] = mm_tn(dj[...], a1[:, other_cols]).astype(BF16).reshape(g_send.shape)
        g_copy = send(g_send, g_recv, pair_sems, 0, partner_core)
        g_copy.start()
        host.run(*tail[1])
        g_own[...] = mm_tn(dj[...], a1[:, mine_cols]).astype(BF16).reshape(g_own.shape)
        g_save = pltpu.make_async_copy(g_own, gjoint_out.at[:, core], save_sems.at[1])
        g_save.start()
        host.run(*tail[2])

        for d in range(1, half):
            far_copy(d).wait_recv()
            acc[...] += far_recv[d - 1].astype(F32)
        d_normed = acc[...]
        normal, inverse = norm_stats(x_own[...].astype(F32))
        sums_one_ref[0:1, :] = jnp.sum(d_normed * normal, axis=0, keepdims=True)
        sums_one_ref[1:2, :] = jnp.sum(d_normed, axis=0, keepdims=True)
        d_normal = d_normed * vec_ref[0, LN1_GAIN : LN1_GAIN + 1, :]
        d_in = (
            dh[...]
            + inverse
            * (
                d_normal
                - jnp.mean(d_normal, axis=-1, keepdims=True)
                - normal * jnp.mean(d_normal * normal, axis=-1, keepdims=True)
            )
        ).astype(BF16)
        dx_own[...] = d_in
        dx_copy = send(dx_own, dx_recv, pair_sems, 1, partner_core)
        dx_copy.start()
        dx_save = pltpu.make_async_copy(dx_own, dx_out.at[0], save_sems.at[2])
        dx_save.start()
        host.run(*tail[3])
        g_copy.wait()
        g_save_other = pltpu.make_async_copy(g_recv, gjoint_out.at[:, 1 - core], save_sems.at[3])
        g_save_other.start()
        dx_copy.wait()
        dx_save_other = pltpu.make_async_copy(dx_recv, dx_out.at[1], save_sems.at[4])
        dx_save_other.start()
        for d in range(half):
            core_copy(d).wait_send()
        for d in range(1, half):
            far_copy(d).wait_send()
        for save in (gout_save, g_save, dx_save, g_save_other, dx_save_other):
            save.wait()
        rows_copy.wait()
        host.finish()


def back_call(layer, dy, hidden, wos, vec, upper, a2, ups, downs, given, late, mask, host, arrays):
    rows = dy.shape[1]
    ranks = host.count
    width = D // ranks
    half = ranks // 2
    shards = host.dp_count * ranks
    per = shards // NCH
    unit = FF // shards // 2
    heads = width // DH
    now = lambda i: (0, jnp.minimum(i, NCH - 1))
    whole = lambda i: (0, 0)
    anywhere = pl.BlockSpec(memory_space=pl.ANY)
    times = []
    for i in range(NCH):
        times += [2.9 * i + 1.6, 2.9 * i + 2.9]
    times += [29.0, 33.0, 36.0]
    for i in range(LEN // BQ * heads):
        times.append(36.0 + 28.0 / (LEN // BQ * heads) * (i + 1))
    times += [69.0, 73.0, 76.0, 84.0]
    ranges = host.slots(times)
    piece = pltpu.VMEM((NCH, rows, FC // 2), BF16)
    tokens = pltpu.VMEM((LEN, width), BF16)
    own = pltpu.VMEM((rows, D), BF16)
    view = host.view_shape(host.arrays - 1)
    return pl.pallas_call(
        functools.partial(back_kernel, layer, host, ranges),
        grid=(NCH + 1,),
        in_specs=[
            pl.BlockSpec((rows, FC), now),
            pl.BlockSpec((1, LEN), whole),
            pl.BlockSpec((1, VEC_ROWS, D), lambda i: (layer, 0, 0)),
        ]
        + [anywhere] * (10 + len(late) + len(arrays)),
        out_specs=[
            pl.BlockSpec((1, FC), now),
            pl.BlockSpec((8, D), whole),
            pl.BlockSpec((8, D), whole),
            pl.BlockSpec((8, width), whole),
        ]
        + [anywhere] * 5
        + host.out_specs(),
        out_shape=[
            jax.ShapeDtypeStruct((1, FF), F32),
            jax.ShapeDtypeStruct((8, D), F32),
            jax.ShapeDtypeStruct((8, D), F32),
            jax.ShapeDtypeStruct((8, width), F32),
            jax.ShapeDtypeStruct(view, BF16),
            jax.ShapeDtypeStruct((2, rows, D), BF16),
            jax.ShapeDtypeStruct((3, 2, width, D // 2), BF16),
            jax.ShapeDtypeStruct((D, D // 2), BF16),
            jax.ShapeDtypeStruct((2, rows, D), BF16),
        ]
        + host.out_shapes(),
        scratch_shapes=[
            own,
            pltpu.VMEM((rows, D), F32),
            pltpu.VMEM((2, rows, D), BF16),
            pltpu.VMEM((D, D), BF16),
            pltpu.VMEM((2, D, FC), BF16),
            pltpu.VMEM((2, FC, D), BF16),
            pltpu.SemaphoreType.DMA((4,)),
            pltpu.SemaphoreType.DMA((2, 2)),
            pltpu.VMEM((rows, D), F32),
            piece,
            piece,
            piece,
            pltpu.VMEM((2, per, unit, D), BF16),
            pltpu.VMEM((2, rows, D), BF16),
            pltpu.VMEM((rows, D), F32),
            pltpu.VMEM((ranks, rows, width), BF16),
            tokens,
        ]
        + dma_pair(NCH)
        + dma_pair(ranks + 1)
        + [pltpu.SemaphoreType.DMA((2,)), pltpu.SemaphoreType.DMA((5,))]
        + [pltpu.VMEM(t.shape[1:] if i == 5 else t.shape, t.dtype) for i, t in enumerate(late)]
        + [pltpu.SemaphoreType.DMA((len(late),))]
        + [
            pltpu.VMEM((LEN, width), F32),
            pltpu.VMEM((LEN, width), F32),
            pltpu.VMEM((LEN, 3 * width), BF16),
            pltpu.VMEM((half, rows, D), BF16),
            pltpu.VMEM((half - 1, rows, D), BF16),
            pltpu.VMEM((half - 1, rows, D), BF16),
        ]
        + ([] if ranks == 4 else [pltpu.VMEM((half, rows, D), BF16)])
        + [
            pltpu.VMEM((3, width, D // 2), BF16),
            pltpu.VMEM((3, width, D // 2), BF16),
            pltpu.VMEM((3, width, D // 2), BF16),
            pltpu.VMEM((D, D // 2), BF16),
            own,
        ]
        + dma_pair(half)
        + dma_pair(half - 1)
        + dma_pair(2)
        + deliver_sems()
        + host.scratch(),
        compiler_params=pltpu.CompilerParams(
            vmem_limit_bytes=BACK_LIMIT, collective_id=layer, has_side_effects=True
        ),
        cost_estimate=pl.CostEstimate(
            flops=100 * 10**9, bytes_accessed=60 * 2**20, transcendentals=rows * FF
        ),
    )(
        upper,
        mask,
        vec,
        dy,
        hidden,
        a2,
        wos[0],
        wos[1],
        ups[0],
        ups[1],
        downs[0],
        downs[1],
        given,
        *late,
        *[host.view(i, array) for i, array in enumerate(arrays)],
    )


def final_kernel(host, *refs):
    n = host.arrays
    srcs, rows_src = refs[:n], refs[n]
    outs, rows_out = refs[n + 1 : 2 * n + 1], refs[2 * n + 1]
    rows_sems = refs[2 * n + 2 : 2 * n + 5]
    rows_mine, rows_sem = refs[2 * n + 5 : 2 * n + 7]
    host.bind(srcs, outs, refs[2 * n + 7 :])
    rows_load = pltpu.make_async_copy(rows_src.at[0], rows_mine, rows_sem)
    rows_load.start()
    group = Group()
    group.greet(host.dp_count)
    host.begin()
    rows_copy = Deliver(group, 0, rows_mine, rows_out, rows_sems)
    rows_load.wait()
    rows_copy.start()
    host.run(0, len(host.events))
    host.finish()
    rows_copy.wait()


def final_call(host, arrays, rows_src, collective_id):
    anywhere = pl.BlockSpec(memory_space=pl.ANY)
    return pl.pallas_call(
        functools.partial(final_kernel, host),
        in_specs=[anywhere] * (host.arrays + 1),
        out_specs=[anywhere] * (host.arrays + 1),
        out_shape=host.out_shapes() + [jax.ShapeDtypeStruct(rows_src.shape, BF16)],
        scratch_shapes=deliver_sems()
        + [pltpu.VMEM(rows_src.shape[1:], BF16), pltpu.SemaphoreType.DMA]
        + host.scratch(),
        compiler_params=pltpu.CompilerParams(
            vmem_limit_bytes=VMEM_LIMIT, collective_id=collective_id, has_side_effects=True
        ),
    )(*host.views(arrays), rows_src)


def assemble_kernel(count, *refs):
    refs = list(refs)

    def pop(number):
        taken = refs[:number]
        del refs[:number]
        return taken

    sources = [pop(2) for _ in range(7)]
    row_outs = pop(2)
    up_out, down_out, out_out, joint_out = pop(4)
    vec_outs = pop(9)
    up, down, mixed, joint, little = pop(5)
    sems = pop(1)[0]
    core = lax.axis_index("section")
    half_ranks = count // 2
    compact = half_ranks == 2
    low = lax.rem(lax.axis_index("seq"), half_ranks)
    loads = []
    for i, (pair, target) in enumerate(zip(sources, [up, down, mixed, joint, little] + row_outs)):
        if i == 4:
            lines = little.shape[1]
            pair = [one.at[:, at * lines : (at + 1) * lines] for at, one in enumerate(pair)]
        first = pltpu.make_async_copy(pair[0], target, sems.at[i])
        second = pltpu.make_async_copy(pair[1], target, sems.at[i])
        pl.when(core == 0)(first.start)
        pl.when(core == 1)(second.start)
        loads.append(first)
    unit = up.shape[1]
    half_cols = D // 2
    loads[1].wait()
    for half in range(2):
        for g in range(FF // 2 // unit):
            at = (2 * g + half) * unit
            down_out[:, at : at + unit] = down[half, :, g * unit : (g + 1) * unit]
    loads[0].wait()
    for half in range(2):
        up_out[:, half * unit : (half + 1) * unit] = up[half].T
    for load in loads[2:5]:
        load.wait()
    for half in range(2):
        cols = slice(half * half_cols, (half + 1) * half_cols)
        value = mixed[half]
        if compact:
            heads = half_cols // DH // 2
            pieces = []
            for i in range(heads):
                for j in range(2):
                    at = (j * heads + i) * DH
                    pieces.append(value[:, at : at + DH])
            value = jnp.concatenate(pieces, axis=1)
        out_out[:, cols] = value
        value = joint[half]
        if compact:
            pieces = [value[i * DH : (i + 1) * DH, :] for i in range(4)]
            joint_out[0:DH, cols] = jnp.where(low == 0, pieces[0], pieces[1])
            joint_out[DH : 2 * DH, cols] = pieces[3]
            joint_out[2 * DH : 3 * DH, cols] = jnp.where(low == 0, pieces[1], pieces[2])
        else:
            joint_out[:, cols] = value
    total = little[0] + little[1]
    at = 0
    for out in vec_outs:
        size = out.shape[1]
        for start in range(0, size, 128):
            wide = min(128, size - start)
            row, lane = (at + start) // 128, (at + start) % 128
            out[:, start : start + wide] = total[row : row + 1, lane : lane + wide]
        at += size
    for load in loads[5:]:
        load.wait()


def assemble_call(count, groups, pairs):
    unit = D // groups
    anywhere = pl.BlockSpec(memory_space=pl.ANY)
    vmem = pl.BlockSpec(memory_space=pltpu.VMEM)
    sizes = [unit] * 8 + [FF // groups]
    flat = [array for pair in pairs for array in pair]
    return pl.pallas_call(
        functools.partial(assemble_kernel, count),
        in_specs=[anywhere] * len(flat),
        out_specs=[vmem] * 15,
        out_shape=[jax.ShapeDtypeStruct(pair[0].shape, BF16) for pair in pairs[5:]]
        + [
            jax.ShapeDtypeStruct((D, FF // groups), F32),
            jax.ShapeDtypeStruct((unit, FF), F32),
            jax.ShapeDtypeStruct((unit, D), F32),
            jax.ShapeDtypeStruct((3 * unit, D), F32),
        ]
        + [jax.ShapeDtypeStruct((1, size), F32) for size in sizes],
        scratch_shapes=[pltpu.VMEM(pair[0].shape, F32) for pair in pairs[:4]]
        + [pltpu.VMEM((2, pairs[4][0].shape[1] // 2, 128), F32)]
        + [pltpu.SemaphoreType.DMA((7,))],
        compiler_params=params(),
    )(*flat)


def swap(value, axis, mask):
    count = lax.axis_size(axis)
    return lax.ppermute(value, axis, [(i, i ^ mask) for i in range(count)])


def take(value, index, dim):
    return lax.dynamic_index_in_dim(value, index, dim, keepdims=False)


def ordered(bit, mine, other, dim):
    return jnp.where(
        bit == 0,
        jnp.stack([mine, other], axis=dim),
        jnp.stack([other, mine], axis=dim),
    )


def key_bias(counts, rotate):
    places = jnp.arange(LEN, dtype=jnp.int32)
    places = jnp.where(rotate, (places + LEN // 2) % LEN, places)
    offset = jnp.maximum(places - TRI, 0)
    view_index = offset // VSLOT
    inside = offset - view_index * VSLOT
    match = view_index[:, None] == jnp.arange(VIEWS, dtype=jnp.int32)[None, :]
    limits = jnp.sum(jnp.where(match, counts[None, :], 0), axis=1)
    valid = (places < TRI) | (inside < limits)
    return jnp.where(valid, 0.0, -1e30).astype(F32)[None, :]


def shards(
    inputs,
    cotangent,
    view_tokens,
    ln1_gain,
    ln1_bias,
    w_qkv,
    b_query,
    b_value,
    w_out,
    b_out,
    ln2_gain,
    ln2_bias,
    w_up,
    b_up,
    w_down,
    b_down,
):
    core = lax.axis_index("section")
    place = lax.axis_index("seq")
    dp_index = lax.axis_index("dp")
    count = lax.axis_size("seq")
    dp_count = lax.axis_size("dp")
    groups = dp_count * count
    half = count // 2
    micro = place // half
    low = place % half
    low_bits = half.bit_length() - 1
    rows = inputs.shape[2]
    width = D // count
    rank = core * half + low

    def swap_core(value):
        return swap(value, "section", 1)

    def swap_seq(value, bit):
        return swap(value, "seq", 1 << bit)

    def low_bit(bit):
        return (place >> bit) & 1

    def own_rows(local):
        chunks = local[:, 0]
        far = lax.ppermute(
            take(chunks, 1 - micro, 0),
            ("section", "seq"),
            [(count + z, count + (z ^ half)) for z in range(count)],
        )
        return jnp.where(core == 0, take(chunks, micro, 0), far)

    def gather_rows(own):
        value = own[None]
        for bit in range(low_bits):
            other = swap_seq(value, bit)
            value = ordered(low_bit(bit), value, other, 0).reshape((-1,) + own.shape)
        value = ordered(core, value, swap_core(value), 0)
        return value.reshape((-1,) + own.shape[1:])

    def exchange(value):
        tail = value.shape[1:]
        value = value.reshape((2,) * (low_bits + 1) + tail)
        for bit in range(low_bits):
            dim = low_bits - bit
            mine = take(value, low_bit(bit), dim)
            other = swap_seq(take(value, 1 - low_bit(bit), dim), bit)
            value = ordered(low_bit(bit), mine, other, dim)
        mine = take(value, core, 0)
        other = swap_core(take(value, 1 - core, 0))
        return ordered(core, mine, other, 0).reshape((count,) + tail)

    compact = half == 2
    span = half * width

    def vector_to(value):
        if compact:
            wide = jnp.stack(
                [jnp.where(low == i, value.reshape(len(value), -1, DH), 0.0) for i in range(2)], axis=2
            )
        else:
            wide = jnp.stack([jnp.where(low == i, value, 0.0) for i in range(half)], axis=1)
        wide = wide.reshape(len(value), span)
        return jnp.concatenate([jnp.where(core == i, wide, 0.0) for i in range(2)], axis=1)

    def rank_rows(value):
        if compact:
            value = value.reshape(2, width // DH, 2, DH, D)
            return jnp.swapaxes(value, 1, 2).reshape(D, D)
        return value

    out_mine = rank_rows(w_out[0])
    ups = (w_up[0], swap_core(w_up[0]))
    downs = (w_down[0], swap_core(w_down[0]))
    bias_mask = key_bias(take(view_tokens[:, 0], micro, 0), micro == 1)

    saved = []
    acts = []
    for layer in range(2):
        if layer == 0:
            o_own, lse, a1, q, k, v, layer_in, joint_pair, out_other, vec = attend_call(
                True,
                0,
                bias_mask,
                count,
                dp_count,
                inputs,
                w_qkv,
                out_mine[None],
                ln1_gain,
                ln1_bias,
                b_query,
                b_value,
                b_out,
                ln2_gain,
                ln2_bias,
                b_down,
                b_up,
            )
            outs_pair = (out_mine, out_other)
        else:
            o_own, lse, a1, q, k, v, d_out_all = attend_call(
                False, 1, bias_mask, count, dp_count, layer_in, joint_pair, vec, cotangent
            )
        hidden, upper, output, a2_all, o_all, gated_all, first_rows = mlp_call(
            layer, dp_count, o_own, layer_in, outs_pair, vec, ups, downs
        )
        acts.append(output)
        saved.append((layer_in, a1, q, k, v, lse, hidden, upper, a2_all, o_all, gated_all))
        layer_in = output

    def hosted(arrays, spans=None, shares=STAGE_SHARES, even=False):
        shapes = []
        for array in arrays:
            shapes.append((array.shape[1], array.shape[2], array.shape[0] != groups, array.dtype))
        return Hosted(dp_count, count, tuple(shapes), spans, shares, even)

    results = [{}, {}]
    pending = None
    sums = []
    for layer in (1, 0):
        x_own, a1, q, k, v, lse, hidden, upper, a2_all, o_all, gated_all = saved[layer]
        g_down = mm_tn(d_out_all.reshape(2 * rows, D), gated_all.reshape(2 * rows, FF // 2))
        g_down = g_down.astype(BF16).reshape(groups, D // groups, FF // 2)
        up_like = jax.ShapeDtypeStruct((groups, FF // groups // 2, D), BF16)
        if pending is None:
            arrays = [g_down]
            host = hosted(
                arrays + [up_like],
                ((0, 0.0, 48.0), (1, 28.0, 78.0)),
                (0.4, 0.6, 0.8, 1.0),
                True,
            )
        else:
            arrays = list(pending) + [g_down]
            host = hosted(
                arrays + [up_like],
                ((0, 0.0, 36.0), (0, 0.0, 36.0), (0, 12.0, 80.0), (1, 40.0, 120.0)),
            )
        (g_bup, sums_two, sums_one, sums_qv, g_up, d_in, g_joint, g_out, given, *reduced) = back_call(
            layer,
            d_out_all,
            hidden,
            outs_pair,
            vec,
            upper,
            a2_all,
            ups,
            downs,
            acts[1][None] if pending is None else d_out_all,
            (q, k, v, lse, a1, joint_pair, x_own, o_all),
            bias_mask,
            host,
            arrays,
        )
        if pending is None:
            second_rows = given
        else:
            second_grads = given
            for name in ("out", "joint"):
                results[1][name] = reduced.pop(0)
        results[layer]["down"], results[layer]["up"] = reduced
        g_out = g_out.reshape(groups, D // groups, D // 2)
        if compact:
            g_joint = g_joint.reshape(groups // 2, 3 * D // groups, D // 2)
        else:
            spread = jnp.stack(
                [jnp.where(low == i, g_joint, jnp.zeros_like(g_joint)) for i in range(half)], axis=2
            )
            g_joint = spread.reshape(groups, 3 * D // groups, D // 2)
        sums.append((sums_one, sums_qv, sums_two, g_bup))
        if pending is None:
            pending = (g_out, g_joint)
        else:
            one, qv, two, bup = (jnp.stack([sums[1][i], sums[0][i]]) for i in range(4))
            lines_of = jnp.concatenate(
                [
                    one[:, 0:2],
                    vector_to(qv[:, 0:2].reshape(4, width)).reshape(2, 2, D),
                    two[:, 2:3],
                    two[:, 0:2],
                    two[:, 3:4],
                ],
                axis=1,
            )
            small = jnp.concatenate(
                [
                    jnp.transpose(
                        lines_of.reshape(2, 8, groups, D // groups), (2, 0, 1, 3)
                    ).reshape(groups, 2, -1),
                    jnp.swapaxes(bup.reshape(2, groups, FF // groups), 0, 1),
                ],
                axis=2,
            )
            lines = -(-small.shape[2] // 128)
            lines += -lines % 8
            small = jnp.pad(small, ((0, 0), (0, 0), (0, lines * 128 - small.shape[2])))
            arrays = (g_out, g_joint, small.reshape(groups, 2 * lines, 128))
            out_0, joint_0, small_both, first_grads = final_call(hosted(arrays), arrays, d_in, 4)
            results[0]["out"], results[0]["joint"] = out_0, joint_0
            results[0]["small"] = results[1]["small"] = small_both
        d_out_all = d_in

    pairs = [
        (results[0][name], results[1][name]) for name in ("up", "down", "out", "joint", "small")
    ]
    pairs += [(first_rows, second_rows), (first_grads, second_grads)]
    acts_rows, grad_rows, g_w_up, g_w_down, g_w_out, g_w_qkv, *pieces = assemble_call(
        count, groups, pairs
    )
    g_ln1g, g_ln1b, g_bq, g_bv, g_bo, g_ln2g, g_ln2b, g_bd, g_bup = pieces
    return (
        acts_rows[None, :, None],
        grad_rows[None, :, None],
        g_ln1g,
        g_ln1b,
        g_w_qkv.T[None],
        g_bq,
        g_bv,
        g_w_out.T[None],
        g_bo,
        g_ln2g,
        g_ln2b,
        g_w_up[None],
        g_bup,
        g_w_down.T[None],
        g_bd,
    )


def solution(mesh):
    rows = P(None, "dp", "seq", None)
    vector = P("section", None)
    matrix = P("section", None, None)
    placed = (
        rows,
        rows,
        P(None, "dp", None),
        vector,
        vector,
        matrix,
        vector,
        vector,
        matrix,
        vector,
        vector,
        vector,
        matrix,
        vector,
        matrix,
        vector,
    )
    both = P("section", None, "dp", "seq", None)
    line = P("section", ("dp", "seq"))
    table = P("section", None, ("dp", "seq"))
    return jax.shard_map(
        shards,
        mesh=mesh,
        in_specs=placed,
        out_specs=(
            both,
            both,
            line,
            line,
            table,
            line,
            line,
            table,
            line,
            line,
            line,
            table,
            line,
            table,
            line,
        ),
        check_vma=False,
    )
```

profile of v0, /device:TPU:9, one launch (start us, length us, event | category | flops | bytes accessed | tf_op | source)
XLA Modules:
  0.0 470.7 jit_solution(17443680677061423327)
XLA Ops:
  0.6 0.0 copy-start
  0.7 0.7 collective-permute-start
  1.4 0.1 collective-permute-start.1
  1.5 3.2 copy.39
  4.7 0.1 select_reduce_fusion
  4.8 0.6 or_select_fusion.refs_3_.refs_2_.refs_1_
  5.4 45.0 %shard_map.271 = (bf16[4,320,256]{2,1,0:T(8,128)(2,1)}, f32[1280,128]{1,0:T(8,128)}, bf16[1280,1024]{1,0:T(8,128)(2,1)}, bf16[1280,256]{1,0:T(8,128)(2,1)}, bf16...) custom-call(bf16[2,1,320,1024]{3,2,1,0:T(8,128)(2,1)} %refs_0_.1, ...), custom_call_target="tpu_custom_call" | custom-call | flops 40000000000 | bytes 20971520 | tf_op jit(solution)/shard_map/pallas_call | solution.py:780
  50.5 0.0 collective-permute-done.up1_ref.refs_9_
  50.5 0.0 collective-permute-done.1.down1_ref.refs_11_
  50.5 22.5 %shard_map.272 = (f32[320,1024]{1,0:T(8,128)}, f32[320,4096]{1,0:T(8,128)}, bf16[320,1024]{1,0:T(8,128)(2,1)}, bf16[2,320,1024]{2,1,0:T(8,128)(2,1)}, bf16[2,320...) custom-call(bf16[4,320,256]{2,1,0:T(8,128)(2,1)} %get-tuple-element.86.o_ref, ...), custom_call_target="tpu_custom_call" | custom-call | flops 6039797760 | bytes 31457280 | tf_op jit(solution)/shard_map/pallas_call | solution.py:931
  72.9 42.1 %shard_map.273 = (bf16[4,320,256]{2,1,0:T(8,128)(2,1)}, f32[1280,128]{1,0:T(8,128)}, bf16[1280,1024]{1,0:T(8,128)(2,1)}, bf16[1280,256]{1,0:T(8,128)(2,1)}, bf16...) custom-call(bf16[320,1024]{1,0:T(8,128)(2,1)} %get-tuple-element.91.refs_0_.x_ref.refs_19_, ...), custom_call_target="tpu_custom_call" | custom-call | flops 40000000000 | bytes 20971520 | tf_op jit(solution)/shard_map/pallas_call | solution.py:780
  115.0 23.7 %shard_map.274 = (f32[320,1024]{1,0:T(8,128)}, f32[320,4096]{1,0:T(8,128)}, bf16[320,1024]{1,0:T(8,128)(2,1)}, bf16[2,320,1024]{2,1,0:T(8,128)(2,1)}, bf16[2,320...) custom-call(bf16[4,320,256]{2,1,0:T(8,128)(2,1)} %get-tuple-element.93.o_ref, ...), custom_call_target="tpu_custom_call" | custom-call | flops 6039797760 | bytes 31457280 | tf_op jit(solution)/shard_map/pallas_call | solution.py:931
  138.8 6.8 %bitcast_convert_fusion.1 = bf16[1024,2048]{1,0:T(8,128)(2,1)} fusion(bf16[2,320,1024]{2,1,0:T(8,128)(2,1)S(1)} %copy-done.6, bf16[2,320,2048]{2,1,0:T(8,128)(2,1)} %get-tuple-element.105), kind=kOutput, calls=%fused_computation.1 | convolution fusion | flops 2686451712 | bytes 8126464 | tf_op jit(solution)/shard_map/dot_general | solution.py:44
  145.6 119.2 %shard_map.275 = (f32[1,4096]{1,0:T(1,128)}, f32[8,1024]{1,0:T(8,128)}, f32[8,1024]{1,0:T(8,128)}, f32[8,256]{1,0:T(8,128)}, bf16[2,2,2,2,128,1024]{5,4,3,2,1,0:...) custom-call(f32[320,4096]{1,0:T(8,128)} %get-tuple-element.94.refs_0, ...), custom_call_target="tpu_custom_call" | custom-call | flops 99999997952 | bytes 62914560 | tf_op jit(solution)/shard_map/pallas_call | solution.py:1324
  264.8 7.6 %bitcast_convert_fusion = bf16[1024,2048]{1,0:T(8,128)(2,1)} fusion(bf16[2,320,1024]{2,1,0:T(8,128)(2,1)} %get-tuple-element.106.refs_3_.refs_12_, bf16[2,320,2048]{2,1,0:T(8,128)(2,1)} %get-tuple-element.117), kind=kOutput, calls=%fused_computation | convolution fusion | flops 2686451712 | bytes 8126464 | tf_op jit(solution)/shard_map/dot_general | solution.py:44
  272.4 143.1 %shard_map.276 = (f32[1,4096]{1,0:T(1,128)}, f32[8,1024]{1,0:T(8,128)}, f32[8,1024]{1,0:T(8,128)}, f32[8,256]{1,0:T(8,128)}, bf16[2,2,2,2,128,1024]{5,4,3,2,1,0:...) custom-call(f32[320,4096]{1,0:T(8,128)} %get-tuple-element.90.refs_0, ...), custom_call_target="tpu_custom_call" | custom-call | flops 99999997952 | bytes 62914560 | tf_op jit(solution)/shard_map/pallas_call | solution.py:1324
  415.5 0.7 broadcast_select_fusion.3
  416.3 0.1 select_n.162
  416.3 0.1 select_n.165
  416.5 0.1 select_n.167
  416.6 0.1 select_n.170
  416.7 0.9 pad_maximum_fusion.3
  417.6 0.8 pad_maximum_fusion
  418.3 0.1 concatenate.12
  418.4 0.1 reshape.194
  418.6 0.1 reshape.195
  418.7 0.8 maximum_bitcast_fusion
  419.4 0.1 select_maximum_fusion
  419.5 0.8 reshape_reshape.29.refs_2_
  420.3 44.8 %shard_map.277 = (f32[2,64,512]{2,1,0:T(8,128)}, f32[2,256,512]{2,1,0:T(8,128)}, f32[2,16,128]{2,1,0:T(8,128)}, bf16[2,320,1024]{2,1,0:T(8,128)(2,1)}) custom-call(bf16[2,2,2,2,64,512]{5,4,3,2,1,0:T(8,128)(2,1)} %bitcast.71, bf16[2,2,2,192,512]{4,3,2,1,0:T(8,128)(2,1)} %bitcast.70, f32[2,2,2,2,16,128]{5,4,3,2,1,0:T(8,128)} %reshape_reshape.29.refs_2_, ...), custom_call_target="tpu_custom_call" | custom-call | tf_op jit(solution)/shard_map/pallas_call | solution.py:1445
  465.0 0.0 copy-start.1
  465.0 5.4 %shard_map.278 = (bf16[2,320,1024]{2,1,0:T(8,128)(2,1)}, bf16[2,320,1024]{2,1,0:T(8,128)(2,1)}, f32[1024,256]{1,0:T(8,128)}, f32[64,4096]{1,0:T(8,128)}, f32[64,...) custom-call(f32[2,128,1024]{2,1,0:T(8,128)} %get-tuple-element.118.r, ...), custom_call_target="tpu_custom_call" | custom-call | tf_op jit(solution)/shard_map/pallas_call | solution.py:1538
  (22 shorter events, 0.2 us)
Async XLA Ops:
  0.6 4.0 copy-start
  0.7 49.8 %collective-permute-start = (bf16[1024,4096]{1,0:T(8,128)(2,1)}, bf16[1024,4096]{1,0:T(8,128)(2,1)}, u32[]{:S(2)}, u32[]{:S(2)}) collective-permute-start(bf16[1024,4096]{1,0:T(8,128)(2,1)} %bitcast.54), channel_id=1, source_target_pairs={{0,16},{16,0},{1,17},{17,1},{2,18},{18,2},{3,19},{19,3},{4,20},{20... | collective-permute-start | bytes 25165832 | tf_op jit(solution)/shard_map/ppermute | solution.py:1559
  1.4 49.1 %collective-permute-start.1 = (bf16[4096,1024]{1,0:T(8,128)(2,1)}, bf16[4096,1024]{1,0:T(8,128)(2,1)}, u32[]{:S(2)}, u32[]{:S(2)}) collective-permute-start(bf16[4096,1024]{1,0:T(8,128)(2,1)} %bitcast.59), channel_id=1, source_target_pairs={{0,16},{16,0},{1,17},{17,1},{2,18},{18,2},{3,19},{19,3},{4,20},{20... | collective-permute-start | bytes 25165832 | tf_op jit(solution)/shard_map/ppermute | solution.py:1559
  115.0 23.7 %copy-start.6 = (bf16[2,320,1024]{2,1,0:T(8,128)(2,1)S(1)}, bf16[2,320,1024]{2,1,0:T(8,128)(2,1)}, u32[]{:S(2)}) copy-start(bf16[2,320,1024]{2,1,0:T(8,128)(2,1)} %get-tuple-element.95.refs_3_) | copy-start | bytes 3932164
  272.4 143.1 %copy-start.5 = (f32[8,256]{1,0:T(8,128)S(1)}, f32[8,256]{1,0:T(8,128)}, u32[]{:S(2)}) copy-start(f32[8,256]{1,0:T(8,128)} %get-tuple-element.127) | copy-start | bytes 24580
  272.4 144.3 %copy-start.2 = (f32[8,1024]{1,0:T(8,128)S(1)}, f32[8,1024]{1,0:T(8,128)}, u32[]{:S(2)}) copy-start(f32[8,1024]{1,0:T(8,128)} %get-tuple-element.129) | copy-start | bytes 98308
  272.4 145.1 %copy-start.3 = (f32[8,1024]{1,0:T(8,128)S(1)}, f32[8,1024]{1,0:T(8,128)}, u32[]{:S(2)}) copy-start(f32[8,1024]{1,0:T(8,128)} %get-tuple-element.125) | copy-start | bytes 98308
  272.4 146.3 %copy-start.4 = (f32[1,4096]{1,0:T(1,128)S(1)}, f32[1,4096]{1,0:T(1,128)}, u32[]{:S(2)}) copy-start(f32[1,4096]{1,0:T(1,128)} %get-tuple-element.131) | copy-start | bytes 49156
  465.0 5.4 %copy-start.1 = (s32[2,1,6]{2,1,0:T(1,128)S(1)}, s32[2,1,6]{2,1,0:T(1,128)}, u32[]{:S(2)}) copy-start(s32[2,1,6]{2,1,0:T(1,128)} %param.18) | copy-start | bytes 148
where the time goes:
time: 480 us; the launch traced here: 471 us
  Pallas kernels  446 us (93%)
  matrix products  14.4 us (3%)
    pallas_call x2, Pallas kernels, back_call(): pl.pallas_call(functools.partial(back_kernel, layer, host, ranges), grid=...  262 us
    pallas_call x2, Pallas kernels, attend_call(): pl.pallas_call(functools.partial(attend_kernel, first, layer, dp_count),...  87.1 us
    pallas_call x2, Pallas kernels, mlp_call(): pl.pallas_call(functools.partial(mlp_kernel, layer, dp_count), grid=(NCHF...  46.2 us
    pallas_call x1, Pallas kernels, final_call(): pl.pallas_call(functools.partial(final_kernel, host), in_specs=[anywhere]...  44.8 us
    dot_general x2, matrix products, mm_tn(): lax.dot_general(a, b, (((0,), (0,)), ((), ())), preferred_element_type=F32)  14.4 us
  transfers between devices with their start and end apart: 2, of which 0 were waited for; matrix products, arithmetic and copies ran while one was open for 1% of the time, Pallas kernels for 10%

commit v1 on v0

--- a/solution.py
+++ b/solution.py
@@ -456,6 +456,20 @@
         device_id=device,
         device_id_type=pl.DeviceIdType.MESH,
     )
+
+
+def rows_of_rank(weights, rank, width, half):
+    if half != 2:
+        return weights[pl.ds(rank * width, width), :]
+    base = rank // 2 * (2 * width) + rank % 2 * DH if isinstance(rank, int) else (
+        lax.div(rank, 2) * (2 * width) + lax.rem(rank, 2) * DH
+    )
+    pieces = []
+    for i in range(width // DH):
+        at = base + 2 * i * DH
+        at = at if isinstance(at, int) else pl.multiple_of(at, DH)
+        pieces.append(weights[pl.ds(at, DH), :])
+    return jnp.concatenate(pieces, axis=0)
 
 
 class Deliver:
@@ -867,7 +881,7 @@
         first.wait()
         hidden = x_ref[...].astype(F32) + vec_ref[0, B_OUT : B_OUT + 1, :]
         for group in range(groups):
-            hidden += mm(o_ref[group], wo[group * width : (group + 1) * width, :])
+            hidden += mm(o_ref[group], rows_of_rank(wo, group, width, half))
         h_ref[...] = hidden
         normal, _ = norm_stats(hidden)
         a_mine[...] = (
@@ -1161,8 +1175,7 @@
         wo_load.wait()
 
         def heads_of(to_rank):
-            at = pl.multiple_of(to_rank * width, width)
-            return mm_nt(d_branch, wo[pl.ds(at, width), :]).astype(BF16)
+            return mm_nt(d_branch, rows_of_rank(wo, to_rank, width, half)).astype(BF16)
 
         copies = []
         for dc, d in group.others():
@@ -1666,13 +1679,7 @@
         wide = wide.reshape(len(value), span)
         return jnp.concatenate([jnp.where(core == i, wide, 0.0) for i in range(2)], axis=1)
 
-    def rank_rows(value):
-        if compact:
-            value = value.reshape(2, width // DH, 2, DH, D)
-            return jnp.swapaxes(value, 1, 2).reshape(D, D)
-        return value
-
-    out_mine = rank_rows(w_out[0])
+    out_mine = w_out[0]
     ups = (w_up[0], swap_core(w_up[0]))
     downs = (w_down[0], swap_core(w_down[0]))
     bias_mask = key_bias(take(view_tokens[:, 0], micro, 0), micro == 1)
@@ -1689,7 +1696,7 @@
                 dp_count,
                 inputs,
                 w_qkv,
-                out_mine[None],
+                w_out,
                 ln1_gain,
                 ln1_bias,
                 b_query,

time: 480 us -> 478 us (level)
  transfers between devices with their start and end apart: 2 -> 2, of which waited for: 0 -> 0; matrix products, arithmetic and copies ran while one was open for 1% -> 0% of each run, Pallas kernels for 10% -> 10%
where the time goes in v1:
time: 478 us; the launch traced here: 468 us
  Pallas kernels  447 us (94%)
  matrix products  14.4 us (3%)
    pallas_call x2, Pallas kernels, back_call(): pl.pallas_call(functools.partial(back_kernel, layer, host, ranges), grid=...  262 us
    pallas_call x2, Pallas kernels, attend_call(): pl.pallas_call(functools.partial(attend_kernel, first, layer, dp_count),...  87.8 us
    pallas_call x2, Pallas kernels, mlp_call(): pl.pallas_call(functools.partial(mlp_kernel, layer, dp_count), grid=(NCHF...  46.6 us
    pallas_call x1, Pallas kernels, final_call(): pl.pallas_call(functools.partial(final_kernel, host), in_specs=[anywhere]...  44.8 us
    dot_general x2, matrix products, mm_tn(): lax.dot_general(a, b, (((0,), (0,)), ((), ())), preferred_element_type=F32)  14.4 us
  transfers between devices with their start and end apart: 2, of which 0 were waited for; matrix products, arithmetic and copies ran while one was open for 0% of the time, Pallas kernels for 10%

profile of v1, /device:TPU:9, one launch (start us, length us, event | category | flops | bytes accessed | tf_op | source)
XLA Modules:
  0.0 468.5 jit_solution(6635305248569403845)
XLA Ops:
  0.6 0.0 copy-start
  0.7 0.7 collective-permute-start
  1.4 0.1 collective-permute-start.1
  1.5 0.1 select_reduce_fusion
  1.6 0.6 or_select_fusion.refs_3_.refs_2_.refs_1_
  2.2 45.9 %shard_map.271 = (bf16[4,320,256]{2,1,0:T(8,128)(2,1)}, f32[1280,128]{1,0:T(8,128)}, bf16[1280,1024]{1,0:T(8,128)(2,1)}, bf16[1280,256]{1,0:T(8,128)(2,1)}, bf16...) custom-call(bf16[2,1,320,1024]{3,2,1,0:T(8,128)(2,1)} %refs_0_.1, ...), custom_call_target="tpu_custom_call" | custom-call | flops 40000000000 | bytes 20971520 | tf_op jit(solution)/shard_map/pallas_call | solution.py:794
  48.2 0.0 collective-permute-done.up1_ref.refs_9_
  48.2 0.0 collective-permute-done.1.down1_ref.refs_11_
  48.2 22.9 %shard_map.272 = (f32[320,1024]{1,0:T(8,128)}, f32[320,4096]{1,0:T(8,128)}, bf16[320,1024]{1,0:T(8,128)(2,1)}, bf16[2,320,1024]{2,1,0:T(8,128)(2,1)}, bf16[2,320...) custom-call(bf16[4,320,256]{2,1,0:T(8,128)(2,1)} %get-tuple-element.86.o_ref, ...), custom_call_target="tpu_custom_call" | custom-call | flops 6039797760 | bytes 31457280 | tf_op jit(solution)/shard_map/pallas_call | solution.py:945
  71.1 41.8 %shard_map.273 = (bf16[4,320,256]{2,1,0:T(8,128)(2,1)}, f32[1280,128]{1,0:T(8,128)}, bf16[1280,1024]{1,0:T(8,128)(2,1)}, bf16[1280,256]{1,0:T(8,128)(2,1)}, bf16...) custom-call(bf16[320,1024]{1,0:T(8,128)(2,1)} %get-tuple-element.91.refs_0_.x_ref.refs_19_, ...), custom_call_target="tpu_custom_call" | custom-call | flops 40000000000 | bytes 20971520 | tf_op jit(solution)/shard_map/pallas_call | solution.py:794
  112.9 0.0 copy-start.6
  112.9 23.7 %shard_map.274 = (f32[320,1024]{1,0:T(8,128)}, f32[320,4096]{1,0:T(8,128)}, bf16[320,1024]{1,0:T(8,128)(2,1)}, bf16[2,320,1024]{2,1,0:T(8,128)(2,1)}, bf16[2,320...) custom-call(bf16[4,320,256]{2,1,0:T(8,128)(2,1)} %get-tuple-element.93.o_ref, ...), custom_call_target="tpu_custom_call" | custom-call | flops 6039797760 | bytes 31457280 | tf_op jit(solution)/shard_map/pallas_call | solution.py:945
  136.7 6.8 %bitcast_convert_fusion.1 = bf16[1024,2048]{1,0:T(8,128)(2,1)} fusion(bf16[2,320,1024]{2,1,0:T(8,128)(2,1)S(1)} %copy-done.6, bf16[2,320,2048]{2,1,0:T(8,128)(2,1)} %get-tuple-element.105), kind=kOutput, calls=%fused_computation.1 | convolution fusion | flops 2686451712 | bytes 8126464 | tf_op jit(solution)/shard_map/dot_general | solution.py:44
  143.5 119.1 %shard_map.275 = (f32[1,4096]{1,0:T(1,128)}, f32[8,1024]{1,0:T(8,128)}, f32[8,1024]{1,0:T(8,128)}, f32[8,256]{1,0:T(8,128)}, bf16[2,2,2,2,128,1024]{5,4,3,2,1,0:...) custom-call(f32[320,4096]{1,0:T(8,128)} %get-tuple-element.94.refs_0, ...), custom_call_target="tpu_custom_call" | custom-call | flops 99999997952 | bytes 62914560 | tf_op jit(solution)/shard_map/pallas_call | solution.py:1337
  262.6 7.6 %bitcast_convert_fusion = bf16[1024,2048]{1,0:T(8,128)(2,1)} fusion(bf16[2,320,1024]{2,1,0:T(8,128)(2,1)} %get-tuple-element.106.refs_3_.refs_12_, bf16[2,320,2048]{2,1,0:T(8,128)(2,1)} %get-tuple-element.117), kind=kOutput, calls=%fused_computation | convolution fusion | flops 2686451712 | bytes 8126464 | tf_op jit(solution)/shard_map/dot_general | solution.py:44
  270.3 143.0 %shard_map.276 = (f32[1,4096]{1,0:T(1,128)}, f32[8,1024]{1,0:T(8,128)}, f32[8,1024]{1,0:T(8,128)}, f32[8,256]{1,0:T(8,128)}, bf16[2,2,2,2,128,1024]{5,4,3,2,1,0:...) custom-call(f32[320,4096]{1,0:T(8,128)} %get-tuple-element.90.refs_0, ...), custom_call_target="tpu_custom_call" | custom-call | flops 99999997952 | bytes 62914560 | tf_op jit(solution)/shard_map/pallas_call | solution.py:1337
  413.3 0.7 broadcast_select_fusion.3
  414.0 0.1 select_n.162
  414.1 0.1 select_n.165
  414.2 0.1 select_n.167
  414.3 0.1 select_n.170
  414.4 0.9 pad_maximum_fusion.3
  415.3 0.8 pad_maximum_fusion
  416.1 0.1 concatenate.12
  416.2 0.1 reshape.190
  416.3 0.1 reshape.191
  416.4 0.8 maximum_bitcast_fusion
  417.2 0.1 select_maximum_fusion
  417.2 0.8 reshape_reshape.29.refs_2_
  418.0 44.8 %shard_map.277 = (f32[2,64,512]{2,1,0:T(8,128)}, f32[2,256,512]{2,1,0:T(8,128)}, f32[2,16,128]{2,1,0:T(8,128)}, bf16[2,320,1024]{2,1,0:T(8,128)(2,1)}) custom-call(bf16[2,2,2,2,64,512]{5,4,3,2,1,0:T(8,128)(2,1)} %bitcast.64, bf16[2,2,2,192,512]{4,3,2,1,0:T(8,128)(2,1)} %bitcast.63, f32[2,2,2,2,16,128]{5,4,3,2,1,0:T(8,128)} %reshape_reshape.29.refs_2_, ...), custom_call_target="tpu_custom_call" | custom-call | tf_op jit(solution)/shard_map/pallas_call | solution.py:1458
  462.8 0.0 copy-start.1
  462.8 5.4 %shard_map.278 = (bf16[2,320,1024]{2,1,0:T(8,128)(2,1)}, bf16[2,320,1024]{2,1,0:T(8,128)(2,1)}, f32[1024,256]{1,0:T(8,128)}, f32[64,4096]{1,0:T(8,128)}, f32[64,...) custom-call(f32[2,128,1024]{2,1,0:T(8,128)} %get-tuple-element.118.r, ...), custom_call_target="tpu_custom_call" | custom-call | tf_op jit(solution)/shard_map/pallas_call | solution.py:1551
  (21 shorter events, 0.1 us)
Async XLA Ops:
  0.6 0.8 copy-start
  0.7 47.5 %collective-permute-start = (bf16[1024,4096]{1,0:T(8,128)(2,1)}, bf16[1024,4096]{1,0:T(8,128)(2,1)}, u32[]{:S(2)}, u32[]{:S(2)}) collective-permute-start(bf16[1024,4096]{1,0:T(8,128)(2,1)} %bitcast.49), channel_id=1, source_target_pairs={{0,16},{16,0},{1,17},{17,1},{2,18},{18,2},{3,19},{19,3},{4,20},{20... | collective-permute-start | bytes 25165832 | tf_op jit(solution)/shard_map/ppermute | solution.py:1572
  1.4 46.8 %collective-permute-start.1 = (bf16[4096,1024]{1,0:T(8,128)(2,1)}, bf16[4096,1024]{1,0:T(8,128)(2,1)}, u32[]{:S(2)}, u32[]{:S(2)}) collective-permute-start(bf16[4096,1024]{1,0:T(8,128)(2,1)} %bitcast.54), channel_id=1, source_target_pairs={{0,16},{16,0},{1,17},{17,1},{2,18},{18,2},{3,19},{19,3},{4,20},{20... | collective-permute-start | bytes 25165832 | tf_op jit(solution)/shard_map/ppermute | solution.py:1572
  112.9 23.7 %copy-start.6 = (bf16[2,320,1024]{2,1,0:T(8,128)(2,1)S(1)}, bf16[2,320,1024]{2,1,0:T(8,128)(2,1)}, u32[]{:S(2)}) copy-start(bf16[2,320,1024]{2,1,0:T(8,128)(2,1)} %get-tuple-element.95.refs_3_) | copy-start | bytes 3932164
  270.3 143.0 %copy-start.5 = (f32[8,256]{1,0:T(8,128)S(1)}, f32[8,256]{1,0:T(8,128)}, u32[]{:S(2)}) copy-start(f32[8,256]{1,0:T(8,128)} %get-tuple-element.127) | copy-start | bytes 24580
  270.3 144.2 %copy-start.2 = (f32[8,1024]{1,0:T(8,128)S(1)}, f32[8,1024]{1,0:T(8,128)}, u32[]{:S(2)}) copy-start(f32[8,1024]{1,0:T(8,128)} %get-tuple-element.129) | copy-start | bytes 98308
  270.3 145.0 %copy-start.3 = (f32[8,1024]{1,0:T(8,128)S(1)}, f32[8,1024]{1,0:T(8,128)}, u32[]{:S(2)}) copy-start(f32[8,1024]{1,0:T(8,128)} %get-tuple-element.125) | copy-start | bytes 98308
  270.3 146.1 %copy-start.4 = (f32[1,4096]{1,0:T(1,128)S(1)}, f32[1,4096]{1,0:T(1,128)}, u32[]{:S(2)}) copy-start(f32[1,4096]{1,0:T(1,128)} %get-tuple-element.131) | copy-start | bytes 49156
  462.8 5.4 %copy-start.1 = (s32[2,1,6]{2,1,0:T(1,128)S(1)}, s32[2,1,6]{2,1,0:T(1,128)}, u32[]{:S(2)}) copy-start(s32[2,1,6]{2,1,0:T(1,128)} %param.18) | copy-start | bytes 148
